TPU v7x, 32 devices: a whole 2x2x4 slice. The times are simulated.
32 devices in a mesh: seq: 16 (over z, x, core), head: 2 (over y).
Axes of the slice: x: 2, y: 2, z: 4, core: 2. Of those that a mesh axis runs over, the one named last changes fastest.
Arguments:
- tokens: bfloat16 [16384, 1152], P(('seq', 'head')), may hold values from -6 to 6
- cotangent: bfloat16 [16384, 1152], P(('seq', 'head')), may hold values from -6 to 6
- buckets: int32 [16], P('seq'), may hold values from 0 to 7
- timesteps: int32 [16], P('seq'), may hold values from 0 to 999
- labels: int32 [16], P('seq'), may hold values from 0 to 999
- class_table: bfloat16 [1000, 1152], replicated, may hold values from -6 to 6
- step_count: int32 [], replicated, may hold values from 2 to 20
- modulate_master: float32 [1152, 6912], P('seq', 'head'), may hold values from -0.1875 to 0.1875
- modulate_first: float32 [1152, 6912], P('seq', 'head'), may hold values from -0.0008544922 to 0.0008544922
- modulate_second: float32 [1152, 6912], P('seq', 'head'), may hold values from 2.049866e-08 to 8.199464e-08
- attend_master: float32 [1152, 3456], P('seq', 'head'), may hold values from -0.1875 to 0.1875
- attend_first: float32 [1152, 3456], P('seq', 'head'), may hold values from -0.00048828125 to 0.00048828125
- attend_second: float32 [1152, 3456], P('seq', 'head'), may hold values from 6.6934405e-09 to 2.6773762e-08
- project_master: float32 [1152, 1152], P('seq', 'head'), may hold values from -0.1875 to 0.1875
- project_first: float32 [1152, 1152], P('seq', 'head'), may hold values from -0.0012207031 to 0.0012207031
- project_second: float32 [1152, 1152], P('seq', 'head'), may hold values from 4.1834003e-08 to 1.6733601e-07
- expand_master: float32 [1152, 4608], P('seq', 'head'), may hold values from -0.1875 to 0.1875
- expand_first: float32 [1152, 4608], P('seq', 'head'), may hold values from -0.0007324219 to 0.0007324219
- expand_second: float32 [1152, 4608], P('seq', 'head'), may hold values from 1.5060241e-08 to 6.0240964e-08
- reduce_master: float32 [4608, 1152], P('seq', 'head'), may hold values from -0.09375 to 0.09375
- reduce_first: float32 [4608, 1152], P('seq', 'head'), may hold values from -0.0012207031 to 0.0012207031
- reduce_second: float32 [4608, 1152], P('seq', 'head'), may hold values from 4.1834003e-08 to 1.6733601e-07
- biases_master: float32 [16128], replicated, may hold values from -1 to 1
- biases_first: float32 [16128], replicated, may hold values from -0.0009765625 to 0.0009765625
- biases_second: float32 [16128], replicated, may hold values from 2.6773762e-08 to 1.0709505e-07
Outputs:
- output: bfloat16 [16384, 1152], P(('seq', 'head'))
- input_grad: float32 [16384, 1152], P(('seq', 'head'))
- grad_norm: float32 [], replicated
- modulate_updated: float32 [1152, 6912], P('seq', 'head')
- modulate_momentum: float32 [1152, 6912], P('seq', 'head')
- modulate_variance: float32 [1152, 6912], P('seq', 'head')
- attend_updated: float32 [1152, 3456], P('seq', 'head')
- attend_momentum: float32 [1152, 3456], P('seq', 'head')
- attend_variance: float32 [1152, 3456], P('seq', 'head')
- project_updated: float32 [1152, 1152], P('seq', 'head')
- project_momentum: float32 [1152, 1152], P('seq', 'head')
- project_variance: float32 [1152, 1152], P('seq', 'head')
- expand_updated: float32 [1152, 4608], P('seq', 'head')
- expand_momentum: float32 [1152, 4608], P('seq', 'head')
- expand_variance: float32 [1152, 4608], P('seq', 'head')
- reduce_updated: float32 [4608, 1152], P('seq', 'head')
- reduce_momentum: float32 [4608, 1152], P('seq', 'head')
- reduce_variance: float32 [4608, 1152], P('seq', 'head')
- biases_updated: float32 [16128], replicated
- biases_momentum: float32 [16128], replicated
- biases_variance: float32 [16128], replicated
All inputs are finite; a program needn't handle non-finite values.
Results may differ from a plain program's by a relative error of at most 0.035.
Values may be sent and summed in bfloat16 or wider, within the bound.
A program may use at most 256 MiB of HBM per device.

v0:
```python
import functools
import math

import jax
import jax.numpy as jnp
from jax import lax
from jax.experimental import pallas as pl
from jax.experimental.pallas import tpu as pltpu
from jax.sharding import Mesh
from jax.sharding import PartitionSpec as P

D = 1152
HEAD_DIM = 72
FF = 4608
SIDE = 32
LMAX = 1024


highest = lax.Precision.HIGHEST
row_units = (8, 4, 16, 6, 10, 7, 4, 6)
col_units = (8, 16, 4, 10, 6, 9, 8, 6)


def table_pick(indices, entries):
    matches = indices[..., None] == jnp.arange(len(entries), dtype=jnp.int32)
    return jnp.sum(jnp.where(matches, jnp.array(entries, jnp.int32), 0), axis=-1)


def layer_norm(value):
    average = jnp.mean(value, axis=-1, keepdims=True)
    centred = value - average
    spread = jnp.mean(centred * centred, axis=-1, keepdims=True)
    return centred * lax.rsqrt(spread + 1e-06)


def modulate(value, shift, scaling):
    return layer_norm(value) * (1.0 + scaling) + shift


def time_features(moments, width):
    half_width = width // 2
    frequency = jnp.exp(-math.log(10000.0) * jnp.arange(half_width, dtype=jnp.float32) / half_width)
    angles = moments.astype(jnp.float32)[:, None] * frequency[None, :]
    return jnp.concatenate([jnp.cos(angles), jnp.sin(angles)], axis=1)


def grid_features(position, row_wide, width):
    quarter = width // 4
    omegas = jnp.exp(-math.log(10000.0) * jnp.arange(quarter, dtype=jnp.float32) / quarter)
    row_angle = (position // row_wide).astype(jnp.float32)[:, None] * omegas[None, :]
    col_angle = (position % row_wide).astype(jnp.float32)[:, None] * omegas[None, :]
    return jnp.concatenate(
        [jnp.sin(row_angle), jnp.cos(row_angle), jnp.sin(col_angle), jnp.cos(col_angle)], axis=1
    )


def fold_rows(left_side, weight_slab):
    return jnp.dot(
        left_side,
        lax.all_gather(weight_slab, "seq", axis=0, tiled=True),
        preferred_element_type=jnp.float32,
    )


def back_cols(gradient, weight_slab):
    return lax.dot_general(
        gradient,
        lax.all_gather(weight_slab, "seq", axis=0, tiled=True),
        (((1,), (1,)), ((), ())),
        preferred_element_type=jnp.float32,
    )


def rows_seq(left_side, right_side):
    return lax.psum_scatter(
        lax.dot_general(
            left_side, right_side, (((0,), (0,)), ((), ())), preferred_element_type=jnp.float32
        ).astype(jnp.bfloat16),
        "seq",
        scatter_dimension=0,
        tiled=True,
    ).astype(jnp.float32)


def attend(queries, key_rows, value_rows, lengths):
    heads_here = queries.shape[1] // HEAD_DIM
    block_rows = min(512, LMAX)
    score_scale = HEAD_DIM ** (-0.5)
    image_count = lengths.shape[0]

    def per_image(packed):
        query_image, key_image, value_image, length = packed
        key_heads = key_image.reshape(LMAX, heads_here, HEAD_DIM)
        value_heads = value_image.reshape(LMAX, heads_here, HEAD_DIM)
        live_keys = jnp.arange(LMAX, dtype=jnp.int32) < length

        def per_block(query_block):
            scores = (
                jnp.einsum(
                    "qhe,khe->hqk", query_block, key_heads, preferred_element_type=jnp.float32
                )
                * score_scale
            )
            scores = jnp.where(live_keys[None, None, :], scores, -1e30)
            maximum = jnp.max(scores, axis=-1, keepdims=True)
            weights = jnp.exp(scores - maximum)
            totals = jnp.sum(weights, axis=-1, keepdims=True)
            probability = (weights / totals).astype(jnp.bfloat16)
            result = jnp.einsum(
                "hqk,khe->qhe", probability, value_heads, preferred_element_type=jnp.float32
            )
            return (result.astype(jnp.bfloat16), (maximum + jnp.log(totals))[:, :, 0])

        blocks = query_image.reshape(LMAX // block_rows, block_rows, heads_here, HEAD_DIM)
        result, log_sums = lax.map(per_block, blocks)
        return (result.reshape(LMAX, heads_here * HEAD_DIM), log_sums)

    stacked = (
        queries.reshape(image_count, LMAX, -1),
        key_rows.reshape(image_count, LMAX, -1),
        value_rows.reshape(image_count, LMAX, -1),
        lengths,
    )
    result, log_sums = lax.map(per_image, stacked)
    return (result.reshape(image_count * LMAX, -1), log_sums)


def attend_back(queries, key_rows, value_rows, grad_rows, log_sums, lengths):
    heads_here = queries.shape[1] // HEAD_DIM
    block_rows = min(512, LMAX)
    score_scale = HEAD_DIM ** (-0.5)
    image_count = lengths.shape[0]

    def per_image(packed):
        query_image, key_image, value_image, grad_image, logsum_image, length = packed
        key_heads = key_image.reshape(LMAX, heads_here, HEAD_DIM)
        value_heads = value_image.reshape(LMAX, heads_here, HEAD_DIM)
        live_keys = jnp.arange(LMAX, dtype=jnp.int32) < length

        def per_block(running, inputs):
            key_grad, value_grad = running
            query_block, grad_block, logsum_block = inputs
            scores = (
                jnp.einsum(
                    "qhe,khe->hqk", query_block, key_heads, preferred_element_type=jnp.float32
                )
                * score_scale
            )
            scores = jnp.where(live_keys[None, None, :], scores, -1e30)
            probability = jnp.exp(scores - logsum_block[:, :, None])
            grad_prob = jnp.einsum(
                "qhe,khe->hqk", grad_block, value_heads, preferred_element_type=jnp.float32
            )
            inner_sum = jnp.sum(probability * grad_prob, axis=-1, keepdims=True)
            grad_score = (probability * (grad_prob - inner_sum)).astype(jnp.bfloat16)
            query_grad = (
                jnp.einsum(
                    "hqk,khe->qhe", grad_score, key_heads, preferred_element_type=jnp.float32
                )
                * score_scale
            )
            key_grad = (
                key_grad
                + jnp.einsum(
                    "hqk,qhe->khe", grad_score, query_block, preferred_element_type=jnp.float32
                )
                * score_scale
            )
            value_grad = value_grad + jnp.einsum(
                "hqk,qhe->khe",
                probability.astype(jnp.bfloat16),
                grad_block,
                preferred_element_type=jnp.float32,
            )
            return ((key_grad, value_grad), query_grad.astype(jnp.bfloat16))

        initial = (
            jnp.zeros((LMAX, heads_here, HEAD_DIM), jnp.float32),
            jnp.zeros((LMAX, heads_here, HEAD_DIM), jnp.float32),
        )
        blocks = (
            query_image.reshape(LMAX // block_rows, block_rows, heads_here, HEAD_DIM),
            grad_image.reshape(LMAX // block_rows, block_rows, heads_here, HEAD_DIM),
            logsum_image,
        )
        (key_grad, value_grad), query_grad = lax.scan(per_block, initial, blocks)
        return (
            query_grad.reshape(LMAX, -1),
            key_grad.reshape(LMAX, -1).astype(jnp.bfloat16),
            value_grad.reshape(LMAX, -1).astype(jnp.bfloat16),
        )

    stacked = (
        queries.reshape(image_count, LMAX, -1),
        key_rows.reshape(image_count, LMAX, -1),
        value_rows.reshape(image_count, LMAX, -1),
        grad_rows.reshape(image_count, LMAX, -1),
        log_sums,
        lengths,
    )
    query_grad, key_grad, value_grad = lax.map(per_image, stacked)
    return (
        query_grad.reshape(image_count * LMAX, -1),
        key_grad.reshape(image_count * LMAX, -1),
        value_grad.reshape(image_count * LMAX, -1),
    )


def adam_update(master, first_moment, second_moment, gradient, learn_rate, clip_factor, correction):
    clipped = gradient * clip_factor
    first_new = 0.5 * first_moment + 0.5 * clipped
    second_new = 0.5 * second_moment + 0.5 * clipped * clipped
    direction = first_new / correction / (jnp.sqrt(second_new / correction) + 1e-08)
    return (master - learn_rate * (direction + 0.1 * master), first_new, second_new)


def on_device(
    tokens,
    cotangent,
    buckets,
    timesteps,
    labels,
    class_table,
    step_count,
    modulate_master,
    modulate_first,
    modulate_second,
    attend_master,
    attend_first,
    attend_second,
    project_master,
    project_first,
    project_second,
    expand_master,
    expand_first,
    expand_second,
    reduce_master,
    reduce_first,
    reduce_second,
    biases_master,
    biases_first,
    biases_second,
):
    head_index = lax.axis_index("head")
    head_count = lax.axis_size("head")
    tok_rows = tokens.shape[0]
    image_count = buckets.shape[0]
    unit_cells = SIDE // 8
    heights = table_pick(buckets, row_units) * unit_cells
    widths = table_pick(buckets, col_units) * unit_cells
    lengths = heights * widths
    row_index = head_index * tok_rows + jnp.arange(tok_rows, dtype=jnp.int32)
    image_of = row_index // LMAX
    position = row_index % LMAX
    choose = image_of[:, None] == jnp.arange(image_count, dtype=jnp.int32)[None, :]
    pick_rows = choose.astype(jnp.float32)
    row_wide = jnp.sum(jnp.where(choose, widths[None, :], 0), axis=1)
    row_length = jnp.sum(jnp.where(choose, lengths[None, :], 0), axis=1)
    live_rows = (position < row_length).astype(jnp.float32)
    grid_cells = grid_features(position, row_wide, D)
    class_pick = (
        labels[:, None] == jnp.arange(class_table.shape[0], dtype=jnp.int32)[None, :]
    ).astype(jnp.bfloat16)
    class_rows = jnp.dot(class_pick, class_table, preferred_element_type=jnp.float32)
    condition = jax.nn.silu(class_rows + time_features(timesteps, D)).astype(jnp.bfloat16)
    bias_low = biases_master.astype(jnp.bfloat16).astype(jnp.float32)
    offset_base = 6 * D
    bias_query = bias_low[offset_base : offset_base + D]
    bias_value = bias_low[offset_base + D : offset_base + 2 * D]
    bias_proj = bias_low[offset_base + 2 * D : offset_base + 3 * D]
    bias_hidden = bias_low[offset_base + 3 * D : offset_base + 3 * D + FF]
    bias_output = bias_low[offset_base + 3 * D + FF :]
    head_slabs = (
        lax.all_gather(attend_master.astype(jnp.bfloat16), "head", axis=1, tiled=True),
        lax.all_gather(project_master.astype(jnp.bfloat16), "head", axis=1, tiled=True),
        lax.all_gather(expand_master.astype(jnp.bfloat16), "head", axis=1, tiled=True),
        lax.all_gather(reduce_master.astype(jnp.bfloat16), "head", axis=1, tiled=True),
    )
    attend_slab, project_slab, expand_slab, reduce_slab = head_slabs
    mod_width = 6 * D // head_count
    mod_share = fold_rows(condition, modulate_master.astype(jnp.bfloat16))
    mod_share = mod_share + lax.dynamic_slice_in_dim(bias_low, head_index * mod_width, mod_width)
    modulation = lax.all_gather(mod_share, "head", axis=1, tiled=True)
    mod_rows = jnp.dot(pick_rows, modulation, precision=highest)
    shift_one, scale_one, gating_one, shift_two, scale_two, gating_two = jnp.split(
        mod_rows, 6, axis=1
    )
    residual_zero = tokens.astype(jnp.float32) + grid_cells
    hidden_attend = modulate(residual_zero, shift_one, scale_one).astype(jnp.bfloat16)
    packed = fold_rows(hidden_attend, attend_slab)
    queries = (packed[:, :D] + bias_query).astype(jnp.bfloat16)
    key_rows = packed[:, D : 2 * D].astype(jnp.bfloat16)
    value_rows = (packed[:, 2 * D :] + bias_value).astype(jnp.bfloat16)
    query_heads, key_heads, value_heads = (
        lax.all_to_all(queries, "head", split_axis=1, concat_axis=0, tiled=True),
        lax.all_to_all(key_rows, "head", split_axis=1, concat_axis=0, tiled=True),
        lax.all_to_all(value_rows, "head", split_axis=1, concat_axis=0, tiled=True),
    )
    head_out, log_sums = attend(query_heads, key_heads, value_heads, lengths)
    attention = lax.all_to_all(head_out, "head", split_axis=0, concat_axis=1, tiled=True)
    branch_attend = fold_rows(attention, project_slab) + bias_proj
    residual_one = residual_zero + gating_one * branch_attend
    hidden_expand = modulate(residual_one, shift_two, scale_two).astype(jnp.bfloat16)
    widened = fold_rows(hidden_expand, expand_slab) + bias_hidden
    activated = jax.nn.gelu(widened, approximate=True).astype(jnp.bfloat16)
    branch_expand = fold_rows(activated, reduce_slab) + bias_output
    output = (residual_one + gating_two * branch_expand).astype(jnp.bfloat16)
    outer_grad = cotangent.astype(jnp.float32) * live_rows[:, None]
    gating_later = outer_grad * branch_expand
    closing_grad = (outer_grad * gating_two).astype(jnp.bfloat16)
    active_grad = back_cols(closing_grad, reduce_slab)
    gelu_value, gelu_pullback = jax.vjp(lambda inner: jax.nn.gelu(inner, approximate=True), widened)
    widened_grad = gelu_pullback(active_grad)[0].astype(jnp.bfloat16)
    hidden_grad = back_cols(widened_grad, expand_slab)
    later_value, later_pullback = jax.vjp(modulate, residual_one, shift_two, scale_two)
    residual_part, shift_later, scale_later = later_pullback(hidden_grad)
    middle_grad = outer_grad + residual_part
    gating_early = middle_grad * branch_attend
    branch_grad = (middle_grad * gating_one).astype(jnp.bfloat16)
    attend_grad = back_cols(branch_grad, project_slab).astype(jnp.bfloat16)
    heads_grad = lax.all_to_all(attend_grad, "head", split_axis=1, concat_axis=0, tiled=True)
    query_grad, keyrow_grad, value_grad = attend_back(
        query_heads, key_heads, value_heads, heads_grad, log_sums, lengths
    )
    query_back, keys_back, values_back = (
        lax.all_to_all(query_grad, "head", split_axis=0, concat_axis=1, tiled=True),
        lax.all_to_all(keyrow_grad, "head", split_axis=0, concat_axis=1, tiled=True),
        lax.all_to_all(value_grad, "head", split_axis=0, concat_axis=1, tiled=True),
    )
    packed_grad = jnp.concatenate([query_back, keys_back, values_back], axis=1)
    normed_grad = back_cols(packed_grad, attend_slab)
    early_value, early_pullback = jax.vjp(modulate, residual_zero, shift_one, scale_one)
    input_part, shift_early, scale_early = early_pullback(normed_grad)
    input_grad = middle_grad + input_part
    mod_token_grad = jnp.concatenate(
        [shift_early, scale_early, gating_early, shift_later, scale_later, gating_later], axis=1
    )
    mod_grad = lax.dot_general(
        pick_rows, mod_token_grad, (((0,), (0,)), ((), ())), precision=highest
    )
    mod_summed = lax.psum_scatter(mod_grad, "head", scatter_dimension=1, tiled=True)
    mod_rounded = mod_summed.astype(jnp.bfloat16)
    grad_mod = rows_seq(condition, mod_rounded)
    mod_slot = lax.dynamic_update_slice_in_dim(
        jnp.zeros((6 * D,), jnp.float32),
        jnp.sum(mod_rounded.astype(jnp.float32), axis=0),
        head_index * mod_width,
        0,
    )
    bias_share = jnp.concatenate(
        [
            mod_slot,
            jnp.sum(query_back.astype(jnp.float32), axis=0),
            jnp.sum(values_back.astype(jnp.float32), axis=0),
            jnp.sum(branch_grad.astype(jnp.float32), axis=0),
            jnp.sum(widened_grad.astype(jnp.float32), axis=0),
            jnp.sum(closing_grad.astype(jnp.float32), axis=0),
        ]
    )
    operand_pairs = (
        (hidden_attend, packed_grad),
        (attention, branch_grad),
        (hidden_expand, widened_grad),
        (activated, closing_grad),
    )
    term_slabs = tuple((rows_seq(left_side, right_side) for left_side, right_side in operand_pairs))
    reduced = (
        lax.psum_scatter(
            term_slabs[0].astype(jnp.bfloat16), "head", scatter_dimension=1, tiled=True
        ).astype(jnp.float32),
        lax.psum_scatter(
            term_slabs[1].astype(jnp.bfloat16), "head", scatter_dimension=1, tiled=True
        ).astype(jnp.float32),
        lax.psum_scatter(
            term_slabs[2].astype(jnp.bfloat16), "head", scatter_dimension=1, tiled=True
        ).astype(jnp.float32),
        lax.psum_scatter(
            term_slabs[3].astype(jnp.bfloat16), "head", scatter_dimension=1, tiled=True
        ).astype(jnp.float32),
    )
    grad_attend, grad_project, grad_expand, grad_reduce = reduced
    local_squares = jnp.sum(grad_mod * grad_mod) + sum(
        (jnp.sum(gradient * gradient) for gradient in reduced)
    )
    bias_total, square_total = lax.psum((bias_share, local_squares), ("seq", "head"))
    grad_norm = jnp.sqrt(square_total + jnp.sum(bias_total * bias_total))
    clip_factor = jnp.minimum(1.0, 1.0 / (grad_norm + 1e-06))
    correction = 1.0 - jnp.power(0.5, step_count.astype(jnp.float32))
    modulate_new = adam_update(
        modulate_master,
        modulate_first,
        modulate_second,
        grad_mod,
        0.5 * D ** (-0.5),
        clip_factor,
        correction,
    )
    attend_new = adam_update(
        attend_master,
        attend_first,
        attend_second,
        grad_attend,
        0.5 * D ** (-0.5),
        clip_factor,
        correction,
    )
    project_new = adam_update(
        project_master,
        project_first,
        project_second,
        grad_project,
        0.5 * D ** (-0.5),
        clip_factor,
        correction,
    )
    expand_new = adam_update(
        expand_master,
        expand_first,
        expand_second,
        grad_expand,
        0.5 * D ** (-0.5),
        clip_factor,
        correction,
    )
    reduce_new = adam_update(
        reduce_master,
        reduce_first,
        reduce_second,
        grad_reduce,
        0.5 * FF ** (-0.5),
        clip_factor,
        correction,
    )
    biases_new = adam_update(
        biases_master, biases_first, biases_second, bias_total, 0.1, clip_factor, correction
    )
    return (
        output,
        input_grad,
        grad_norm,
        modulate_new[0],
        modulate_new[1],
        modulate_new[2],
        attend_new[0],
        attend_new[1],
        attend_new[2],
        project_new[0],
        project_new[1],
        project_new[2],
        expand_new[0],
        expand_new[1],
        expand_new[2],
        reduce_new[0],
        reduce_new[1],
        reduce_new[2],
        biases_new[0],
        biases_new[1],
        biases_new[2],
    )


ALPHA = HEAD_DIM ** (-0.5) * math.log2(math.e)
GELU_A = math.sqrt(2.0 / math.pi)
GELU_B = 0.044715
BLOCK = FF // 16
BF, F32 = jnp.bfloat16, jnp.float32
ANY, VM = pl.ANY, pltpu.VMEM
PIECES = {"q": (144, 864, 48), "p": (72, 576, None), "u": (144, 1152, 48), "d": (288, 576, 96)}
NAMES = ("q", "p", "u", "d")
MESH = pl.DeviceIdType.MESH


def place():
    return tuple(lax.axis_index(a) for a in ("z", "x", "c", "y"))


def at_z(k):
    z = lax.axis_index("z")
    return (z, z + 1 - 2 * (z % 2), (z + 2) % 4, 3 - z)[k]


def rdma(src, dst, send, recv, to):
    return pltpu.make_async_remote_copy(
        src_ref=src, dst_ref=dst, send_sem=send, recv_sem=recv, device_id=to, device_id_type=MESH
    )


def partners():
    z, x, c, y = place()
    xn, yn, twin = (z, 1 - x, c, y), (z, x, c, 1 - y), (z, x, 1 - c, y)
    return xn, yn, twin, [(at_z(k), x, c, y) for k in range(4)]


def flipped(f):
    z, x, c, y = place()
    return (z, 1 - x if f & 1 else x, 1 - c if f & 2 else c, 1 - y if f & 4 else y)


def greet():
    barrier = pltpu.get_barrier_semaphore()
    for to in [flipped(f) for f in range(1, 8)] + partners()[3][1:]:
        pl.semaphore_signal(barrier, inc=1, device_id=to, device_id_type=MESH)
    pl.semaphore_wait(barrier, 10)


CHUNKS = (
    (0, 0, 80, 16),
    (0, 80, 64, 16),
    (1, 0, 72, None),
    (2, 0, 80, 16),
    (2, 80, 64, 16),
    (3, 0, 144, 32),
    (3, 144, 144, 32),
)


def parts_of(chunk, k):
    _, _, rows, cut = CHUNKS[chunk]
    if cut is None:
        return ((0, rows), None) if k == 0 else (None, (0, rows))
    return (0, cut), (cut, rows - cut)


def piece_at(full, w, y, zk, x, first, count):
    rows = PIECES[NAMES[w]][0]
    if count == 72:
        return full.at[y, zk * 2 + x]
    return full.at[y, pl.ds(pl.multiple_of((zk * 2 + x) * rows + first, 16), count)]


def matmul(left, right):
    return jnp.dot(left, right, preferred_element_type=F32)


def matmul_nt(left, right):
    return lax.dot_general(left, right, (((1,), (1,)), ((), ())), preferred_element_type=F32)


def matmul_tn(left, right):
    return lax.dot_general(left, right, (((0,), (0,)), ((), ())), preferred_element_type=F32)


class Gather:
    def __init__(self, own, full, sems):
        self.own, self.full = own, full
        self.zs, self.zr, self.xs, self.xr, self.ys, self.yr, self.fs, self.fr, self.ps, self.pr = sems
        self.sent = []

    def piece(self, w, flip_y, k, flip_x):
        z, x, c, y = place()
        weight, first, count, _ = CHUNKS[w]
        return piece_at(
            self.full[weight], weight, 1 - y if flip_y else y, at_z(k), 1 - x if flip_x else x, first, count
        )

    def source(self, w):
        weight, first, count, _ = CHUNKS[w]
        return self.own[weight].at[pl.ds(first, count)]

    def send(self, make):
        make().start()
        self.sent.append(make)

    def arrived(self, ref, s, r):
        rdma(ref, ref, s, r, partners()[0]).wait_recv()

    def start(self, w):
        def to_x():
            return rdma(self.source(w), self.piece(w, 0, 0, 0), self.xs.at[w, 0], self.xr.at[w, 0], partners()[0])

        def to_y():
            return rdma(self.source(w), self.piece(w, 0, 0, 0), self.ys.at[w, 0], self.yr.at[w, 0], partners()[1])

        def to_z(k):
            to = partners()[3][k]
            return rdma(self.source(w), self.piece(w, 0, 0, 0), self.zs.at[w, k], self.zr.at[w, k], to)

        self.send(to_x)
        self.send(to_y)
        for k in (1, 2, 3):
            self.send(functools.partial(to_z, k))

    def column(self, w, k):
        self.arrived(self.piece(w, 0, k, 0), self.zs.at[w, k], self.zr.at[w, k])

        def to_x():
            piece = self.piece(w, 0, k, 0)
            return rdma(piece, piece, self.xs.at[w, k], self.xr.at[w, k], partners()[0])

        def to_y():
            piece = self.piece(w, 0, k, 0)
            return rdma(piece, piece, self.ys.at[w, k], self.yr.at[w, k], partners()[1])

        self.send(to_x)
        self.send(to_y)

    def plane(self, w, k):
        spans = parts_of(w, k)

        def pass_on(i):
            part = self.piece(w, i, k, 1 - i).at[pl.ds(*spans[i])]
            return rdma(part, part, self.fs.at[w, k, i], self.fr.at[w, k, i], partners()[1 - i])

        self.arrived(self.piece(w, 0, k, 1), self.xs.at[w, k], self.xr.at[w, k])
        if k in (0, 2) and spans[0] is not None:
            self.send(functools.partial(pass_on, 0))
        self.arrived(self.piece(w, 1, k, 0), self.ys.at[w, k], self.yr.at[w, k])
        if k in (0, 2) and spans[1] is not None:
            self.send(functools.partial(pass_on, 1))

    def corner(self, w, k):
        for i, span in enumerate(parts_of(w, k)):
            if span is not None:
                part = self.piece(w, 1, k, 1).at[pl.ds(*span)]
                self.arrived(part, self.fs.at[w, k, i], self.fr.at[w, k, i])

        def to_pair():
            piece = self.piece(w, 1, k, 1)
            return rdma(piece, piece, self.ps.at[w, k], self.pr.at[w, k], partners()[3][1])

        self.send(to_pair)

    def last(self, w, k):
        self.arrived(self.piece(w, 1, k ^ 1, 1), self.ps.at[w, k], self.pr.at[w, k])

    def finish(self):
        for make in self.sent:
            make().wait_send()

    def steps(self):
        def each(method, chunks, ks):
            return [(method, i, k) for i in chunks for k in ks]

        column, plane, corner, last = self.column, self.plane, self.corner, self.last
        one = (0, 1)
        plan = [(self.start, 0), (self.start, 1), (self.start, 2)]
        plan += each(column, one, (1,)) + each(plane, one, (0,))
        plan += each(column, one, (2,)) + each(column, one, (3,)) + [(self.start, 3)]
        plan += each(corner, one, (0,)) + each(plane, one, (2,))
        plan += each(column, (2,), (1,)) + [(self.start, 4)]
        plan += each(plane, one, (1,)) + each(corner, one, (2,))
        plan += each(plane, (2,), (0,)) + each(column, (2,), (2, 3)) + each(column, (3,), (1,))
        plan += each(plane, one, (3,)) + each(last, one, (0, 2))
        count = len(CHUNKS)
        for t in range(-2, count + 4):
            wave = [(self.start, t + 2)] if t + 2 < count else []
            if 0 <= t - 4 < count:
                wave += each(last, (t - 4,), (0, 2))
            for lag, make in enumerate(
                (
                    lambda i: each(column, (i,), (1,)),
                    lambda i: each(plane, (i,), (0,)) + each(column, (i,), (2, 3)),
                    lambda i: each(corner, (i,), (0,)) + each(plane, (i,), (2, 1)),
                    lambda i: each(corner, (i,), (2,)) + each(plane, (i,), (3,)),
                )
            ):
                if t >= 0 and 0 <= t - lag < count:
                    wave += make(t - lag)
            plan += [step for step in wave if step not in plan]
        return plan


def mod_steps(cond_ref, weight, bias, out_ref, lhs, bufs, s, r):
    conds, part, got_z, mid, box = bufs

    def hop(i):
        z, x, c, y = place()
        zn = partners()[3]
        if i == 0:
            pairs = [(conds.at[z, x, c], conds.at[z, x, c], flipped(f)) for f in (1, 2, 3)]
        elif i == 1:
            pairs = [(conds.at[z], conds.at[z], zn[k]) for k in (1, 2, 3)]
        elif i == 2:
            pairs = [(part.at[at_z(k)], got_z.at[k - 1], zn[k]) for k in (1, 2, 3)]
        else:
            pairs = []
            for f in range(1, 8):
                to = flipped(f)
                pairs.append((mid.at[to[1], to[3]], box.at[x, c, y], to))
        return [
            rdma(src, dst, s.at[i, n], r.at[i, n], to) for n, (src, dst, to) in enumerate(pairs)
        ]

    def step(i):
        z, x, c, y = place()
        if i > 0:
            for d in hop(i - 1):
                d.wait()
        if i == 0:
            conds[z, x, c] = cond_ref[...]
        elif i == 2:
            me = (z * 2 + x) * 2 + c
            for n in range(16):
                lhs[pl.ds(n, 1), :] = conds[n // 4, n // 2 % 2, n % 2, pl.ds(me, 1), :]
            for j in range(3):
                cols = slice(j * D, (j + 1) * D)
                result = matmul(lhs[:, :72].astype(BF), weight[:, cols].astype(BF))
                for n in range(16):
                    part[n // 4, n // 2 % 2, n % 2, :, cols] = result[n : n + 1]
        elif i == 3:
            mid[...] = part[z] + got_z[0] + got_z[1] + got_z[2]
            box[x, c, y] = mid[x, y]
        elif i == 4:
            for n in range(2):
                total = (box[0, 0, n] + box[0, 1, n]) + (box[1, 0, n] + box[1, 1, n])
                out_ref[n] = total + bias[:, n * 3456 : (n + 1) * 3456]
        if i < 4:
            for d in hop(i):
                d.start()

    return [functools.partial(step, i) for i in range(5)]


def normed_tile(value):
    average = jnp.mean(value, axis=-1, keepdims=True)
    centred = value - average
    spread = jnp.mean(centred * centred, axis=-1, keepdims=True)
    return centred * lax.rsqrt(spread + 1e-06)


SPACE = (8, 12)


def rounded(value):
    return value.astype(BF).astype(F32)


def pick(bucket, entries):
    return sum(
        jnp.where(bucket == float(i), float(e * (SIDE // 8)), 0.0) for i, e in enumerate(entries)
    )


def start_rows(tok, table, bucket, first, rows):
    wide = pick(bucket, col_units)
    spot = (first + lax.broadcasted_iota(jnp.int32, (rows, 1), 0)).astype(F32)
    lane = lax.broadcasted_iota(jnp.int32, (1, 64), 1).astype(F32)
    grid_row = jnp.where((spot >= lane * wide) & (spot < (lane + 1.0) * wide), 1.0, 0.0)
    left = spot - wide * jnp.sum(grid_row * lane, axis=1, keepdims=True)
    grid_col = jnp.where(left == lane, 1.0, 0.0)
    high = table.astype(BF)
    low = (table - high.astype(F32)).astype(BF)
    parts = [matmul(hot.astype(BF), high) + matmul(hot.astype(BF), low) for hot in (grid_row, grid_col)]
    return tok.astype(F32) + jnp.concatenate(parts, axis=1)


def forward_kernel(*refs):
    (tok, cot, bucket_in, table, att_m, proj_m, exp_m, red_m, mod_w, cond_in, bias_in) = refs[:11]
    gq, gp, gu, gd = full = refs[11:15]
    (mod_out, lhs, x0_out, dy_out, cl_out, h1_out, q_out, k_out, v_out) = refs[15:24]
    (attnt_out, lse_out, ba_out, x1_out, h2_out, der_out, bb_out, y_out, gred_out) = refs[24:33]
    (oq, op, ou, od, fq, tq, fu, tu) = refs[33:41]
    mod_bufs = refs[41:46]
    (xs, x0, dy, bucket, closing, h1, qa, ka, vt, attnt, attn) = refs[46:57]
    (ps, pr, ds, dr, acc, x1, h2, act, der, ba, bb, yo, gstage) = refs[57:70]
    (b_all, b_q, b_v, b_u) = refs[70:74]
    lsem = refs[74]
    gather_sems = refs[75:85]
    ms, mr, ws, wr, ts, tr, os, outs_sem, gsem = refs[85:94]
    z, x, c, y = place()
    xn, yn, twin, zn = partners()
    half = x0.shape[0]
    mine = pl.multiple_of(c * half, half)
    other = pl.multiple_of((1 - c) * half, half)
    gather = Gather((oq, op, ou, od), full, gather_sems)
    mods = mod_steps(cond_in, mod_w, b_all, mod_out, lhs, mod_bufs, ms, mr)
    greet()
    mods[0]()

    def split(master, width, f, t, i):
        count = master.shape[1] // (2 * width)
        sides = [
            jnp.concatenate(
                [master[:, (2 * j + p) * width : (2 * j + p + 1) * width] for j in range(count)], axis=1
            )
            for p in (0, 1)
        ]
        t[...] = jnp.where(c == 0, sides[1], sides[0])
        rdma(t, f.at[c], os.at[0, i], os.at[1, i], twin).start()
        f[c] = jnp.where(c == 0, sides[0], sides[1])

    def joined(f, t, i, piece):
        rdma(t, f.at[c], os.at[0, i], os.at[1, i], twin).wait()
        piece[...] = jnp.concatenate([f[0], f[1]], axis=0).astype(BF)

    steps = [step for step in gather.steps() if step[0] != gather.start or step[1] > 2]
    done = [0]

    def tick(n):
        for f, *a in steps[done[0] : done[0] + n]:
            f(*a)
        done[0] = min(done[0] + n, len(steps))

    def tick_until(chunk):
        last = max(i for i, s in enumerate(steps) if s[0] == gather.last and s[1] == chunk)
        tick(max(0, last + 1 - done[0]))

    swap_to = (z, x, y, c)
    PART = 128
    moves = [(bucket_in, bucket)]
    for i in range(half // PART):
        moves.append((xs.at[pl.ds(i * PART, PART)], x0.at[pl.ds(i * PART, PART)]))
    for i in range(half // PART):
        moves.append((cot.at[pl.ds(i * PART, PART)], dy.at[pl.ds(i * PART, PART)]))

    def move(i):
        @pl.when(c != y)
        def _():
            rdma(*moves[i], ws.at[i], wr.at[i], swap_to).start()

        @pl.when(c == y)
        def _():
            pltpu.make_async_copy(*moves[i], ws.at[i]).start()

    def moved(i):
        @pl.when(c != y)
        def _():
            rdma(*moves[i], ws.at[i], wr.at[i], swap_to).wait()

        @pl.when(c == y)
        def _():
            pltpu.make_async_copy(*moves[i], ws.at[i]).wait()

    def first_rows(i):
        rows = slice(i * PART, (i + 1) * PART)
        xs[rows, :] = start_rows(
            tok[rows, :], table[...], bucket_in[0:1, 0:1], y * half + i * PART, PART
        ).astype(BF)
        move(1 + i)

    move(0)
    split(att_m, HEAD_DIM, fq, tq, 0)
    mods[1]()
    op[...] = proj_m[...].astype(BF)
    gather.start(2)
    first_rows(0)
    joined(fq, tq, 0, oq)
    gather.start(0)
    gather.start(1)
    mods[2]()
    first_rows(1)
    split(exp_m, BLOCK, fu, tu, 1)
    first_rows(2)
    tick(2)
    first_rows(3)
    tick(2)
    joined(fu, tu, 1, ou)
    tick(3)
    mods[3]()
    od[...] = red_m[...].astype(BF)
    owns = [
        pltpu.make_async_copy(
            gather.own[w], piece_at(full[w], w, y, z, x, 0, PIECES[NAMES[w]][0]), lsem.at[w]
        )
        for w in range(4)
    ]
    for d in owns:
        d.start()
    b_all[...] = rounded(bias_in[...]).reshape(1, 14 * D)
    tick(SPACE[0])
    mods[4]()
    tick(SPACE[1])

    def of_core(base, width, count):
        return jnp.concatenate(
            [
                jnp.where(
                    c == 0,
                    b_all[:, base + 2 * j * width : base + (2 * j + 1) * width],
                    b_all[:, base + (2 * j + 1) * width : base + (2 * j + 2) * width],
                )
                for j in range(count)
            ],
            axis=1,
        )

    b_p = b_all.at[:, pl.ds(8 * D, D)]
    b_d = b_all.at[:, pl.ds(9 * D + FF, D)]
    for i in range(1 + half // PART):
        moved(i)

    def vec(i):
        return mod_out[i // 3, :, (i % 3) * D : (i % 3 + 1) * D]

    TILE, WIDE = 128, 256
    tiles = half // TILE

    def own_tile(ref, t):
        return ref.at[pl.ds(pl.multiple_of(mine + t * TILE, TILE), TILE)]

    def give(ref, t, i):
        part = own_tile(ref, t)
        return rdma(part, part, ts.at[i, t], tr.at[i, t], twin)

    def norm_one(t, _):
        rows = pl.ds(pl.multiple_of(t * TILE, TILE), TILE)
        value = normed_tile(x0[rows, :].astype(F32)) * (1.0 + vec(1)) + vec(0)
        own_tile(h1, t)[...] = value.astype(BF)
        give(h1, t, 0).start()
        return 0

    for t in range(tiles):
        norm_one(t, 0)
        tick(1)
    tick_until(1)
    for i in range(half // PART):
        move(1 + half // PART + i)

    def both_got(ref, i):
        for t in range(tiles):
            give(ref, t, i).wait_send()
            part = ref.at[pl.ds(pl.multiple_of(other + t * TILE, TILE), TILE)]
            rdma(part, part, ts.at[i, t], tr.at[i, t], twin).wait_recv()

    out_copies = []

    def put(src, dst):
        d = pltpu.make_async_copy(src, dst, outs_sem.at[len(out_copies)])
        d.start()
        out_copies.append(d)

    def load(src, dst, i):
        d = pltpu.make_async_copy(src, dst, lsem.at[i])
        d.start()
        d.wait()

    owns[0].wait()
    live = pick(bucket[0:1, 0:1], row_units) * pick(bucket[0:1, 0:1], col_units)
    lane = lax.broadcasted_iota(jnp.int32, (1, 128), 1)

    b_q[...] = of_core(6 * D, HEAD_DIM, 8)
    b_v[...] = of_core(7 * D, HEAD_DIM, 8)
    b_u[...] = of_core(9 * D, BLOCK, 8)

    def qkv(weight):
        load(gq, weight, 4)

        def rows_of(start):
            rows = pl.ds(start, half)
            left = h1[rows, :]
            spot = (start + lax.broadcasted_iota(jnp.int32, (half, 1), 0)).astype(F32)
            mask = jnp.where(lane == HEAD_DIM, jnp.where(spot < live, 0.0, -1e30), 0.0)
            ones = jnp.where(lane == HEAD_DIM, 1.0, 0.0)
            fill = jnp.zeros((half, 56), F32)

            def put_key(j, key):
                ka[j, rows, :] = (jnp.concatenate([key, fill], axis=1) + mask).astype(BF)

            one = matmul(left, weight[0])
            for j in range(8):
                cols = slice(j * HEAD_DIM, (j + 1) * HEAD_DIM)
                query = (one[:, cols] + b_q[:, cols]) * ALPHA
                qa[j, rows, :] = (jnp.concatenate([query, fill], axis=1) + ones).astype(BF)
            for j in range(4):
                put_key(j, one[:, 576 + j * 72 : 648 + j * 72])
            tick(2)
            two = matmul(left, weight[1])
            for j in range(4):
                put_key(4 + j, two[:, j * 72 : j * 72 + 72])
            for j in range(8):
                cols = slice(j * HEAD_DIM, (j + 1) * HEAD_DIM)
                value = two[:, 288 + j * 72 : 360 + j * 72] + b_v[:, cols]
                vt[j, :, rows] = value.T.astype(BF)
            tick(2)

        rows_of(mine)
        both_got(h1, 0)
        rows_of(other)

    pl.run_scoped(qkv, VM((2, D, 864), BF))
    put(h1, h1_out)
    tick(1)
    put(qa, q_out)
    put(ka, k_out)
    put(vt, v_out)

    def head(j, _):
        def queries(i, _):
            rows = pl.ds(pl.multiple_of(i * 512, 512), 512)
            scores = matmul_nt(ka[j], qa[j, rows, :])
            top = jnp.max(scores, axis=0, keepdims=True)
            prob = jnp.exp2(scores - top)
            total = jnp.sum(prob, axis=0, keepdims=True)
            result = matmul(vt[j], prob.astype(BF)) * (1.0 / total)
            attnt[j, :, rows] = result
            lse_out[j, :, rows] = top + jnp.log2(total)
            return 0

        lax.fori_loop(0, 2, queries, 0)
        return 0

    for j in range(8):
        head(j, 0)
        tick(3)

    for i in range(half // PART):
        moved(1 + half // PART + i)

    def close(t, _):
        rows = pl.ds(pl.multiple_of(t * TILE, TILE), TILE)
        spot = (mine + t * TILE + lax.broadcasted_iota(jnp.int32, (TILE, 1), 0)).astype(F32)
        outer = jnp.where(spot < live, dy[rows, :].astype(F32), 0.0)
        dy[rows, :] = outer.astype(BF)
        own_tile(closing, t)[...] = (outer * vec(5)).astype(BF)
        give(closing, t, 1).start()
        return 0

    lax.fori_loop(0, tiles, close, 0)
    put(attnt, attnt_out)
    tick_until(2)
    owns[1].wait()

    def proj(weight, stage, raw):
        load(gp, raw, 5)
        for i in (0, 1):
            for h in range(8):
                stage[h * 72 : h * 72 + 72, :] = raw[i, h].astype(F32)
            weight[i] = stage[...].astype(BF)

        def attn_rows(i, _):
            rows = pl.ds(pl.multiple_of(i * 256, 256), 256)
            value = jnp.concatenate([attnt[j, :, rows] for j in range(8)], axis=0)
            attn[rows, :] = value.T.astype(BF)
            return 0

        lax.fori_loop(0, 4, attn_rows, 0)

        def for_twin(t, _):
            rows = pl.ds(pl.multiple_of(t * WIDE, WIDE), WIDE)
            left = attn[pl.ds(pl.multiple_of(other + t * WIDE, WIDE), WIDE), :]
            for i in (0, 1):
                ps[rows, i * 576 : (i + 1) * 576] = matmul(left, weight[i]).astype(BF)
            rdma(ps.at[rows], pr.at[rows], ts.at[2, t], tr.at[2, t], twin).start()
            return 0

        for t in range(half // WIDE):
            for_twin(t, 0)
            tick(1)

        def for_me(t, _):
            rows = pl.ds(pl.multiple_of(t * WIDE, WIDE), WIDE)
            left = attn[pl.ds(pl.multiple_of(mine + t * WIDE, WIDE), WIDE), :]
            for i in (0, 1):
                acc[rows, i * 576 : (i + 1) * 576] = matmul(left, weight[i])
            return 0

        for t in range(half // WIDE):
            for_me(t, 0)
            tick(1)

    pl.run_scoped(proj, VM((2, 576, 576), BF), VM((576, 576), F32), VM((2, 8, 72, 576), BF))

    def middle(t, _):
        rows = pl.ds(pl.multiple_of(t * TILE, TILE), TILE)
        branch = acc[rows, :] + pr[rows, :].astype(F32) + b_p[...]
        ba[rows, :] = branch.astype(BF)
        value = x0[rows, :].astype(F32) + vec(2) * branch
        x1[rows, :] = value
        own_tile(h2, t)[...] = (normed_tile(value) * (1.0 + vec(4)) + vec(3)).astype(BF)
        give(h2, t, 3).start()
        return 0

    def half_got(src, dst, i, t):
        rows = pl.ds(t * WIDE, WIDE)
        rdma(src.at[rows], dst.at[rows], ts.at[i, t], tr.at[i, t], twin).wait()

    for t in range(tiles):
        if t % 2 == 0:
            half_got(ps, pr, 2, t // 2)
        middle(t, 0)
    put(ba, ba_out)
    put(x1, x1_out)
    put(x0, x0_out)
    put(dy, dy_out)
    tick_until(4)
    owns[2].wait()
    both_got(h2, 3)
    both_got(closing, 1)
    put(h2, h2_out)
    put(closing, cl_out)

    def up(weight):
        load(gu, weight, 6)

        def block_of(start, i, n):
            rows = pl.ds(start, half)
            part = slice(n * 384, (n + 1) * 384)
            cols = slice(i * D + n * 384, i * D + (n + 1) * 384)
            u = matmul(h2[rows, :], weight[i, :, part]) + b_u[:, cols]
            square = u * u
            inner = u * (GELU_A + GELU_A * GELU_B * square)
            bent = jnp.tanh(inner)
            half_up = 0.5 + 0.5 * bent
            act[rows, cols] = (u * half_up).astype(BF)
            slope = u * (GELU_A + 3.0 * GELU_A * GELU_B * square)
            der[rows, cols] = (half_up + slope * (half_up * (1.0 - bent))).astype(BF)

        for start in (mine, other):
            for i in (0, 1):
                for n in range(3):
                    block_of(start, i, n)
                    tick(n % 2)

    pl.run_scoped(up, VM((2, D, D), BF))
    put(der, der_out)

    gouts = []
    for t in range(6):
        slot = t % 2
        if t >= 2:
            gouts[t - 2].wait()
        value = matmul(act[:, t * 384 : (t + 1) * 384].T, closing[...])
        for i in (0, 1):
            gstage[slot, i] = value[:, i * 576 : (i + 1) * 576].astype(BF)
        d = pltpu.make_async_copy(
            gstage.at[slot], gred_out.at[:, pl.ds(t * 384, 384)], gsem.at[slot]
        )
        d.start()
        gouts.append(d)
        tick(1)
    for d in gouts[-2:]:
        d.wait()
    tick(len(steps))
    owns[3].wait()

    def down(weight):
        load(gd, weight, 7)

        for i in (0, 1):
            cols = slice(i * 576, (i + 1) * 576)
            ds[:, cols] = matmul(act[pl.ds(other, half), :], weight[i]).astype(BF)
        rdma(ds, dr, ts.at[4, 0], tr.at[4, 0], twin).start()
        for i in (0, 1):
            cols = slice(i * 576, (i + 1) * 576)
            acc[:, cols] = matmul(act[pl.ds(mine, half), :], weight[i])
        rdma(ds, dr, ts.at[4, 0], tr.at[4, 0], twin).wait()

    pl.run_scoped(down, VM((2, 2304, 576), BF))

    def finish(t, _):
        rows = pl.ds(pl.multiple_of(t * TILE, TILE), TILE)
        branch = acc[rows, :] + dr[rows, :].astype(F32) + b_d[...]
        bb[rows, :] = branch.astype(BF)
        yo[rows, :] = (x1[rows, :] + vec(5) * branch).astype(BF)
        return 0

    for t in range(tiles):
        finish(t, 0)
    put(bb, bb_out)
    put(yo, y_out)
    for d in out_copies:
        d.wait()
    gather.finish()


def forward_block(tokens, cotangent, bucket, table, masters, modulate_master, cond, biases):
    shapes = {
        "gq": (2, D, 864),
        "gp": (2, 8, 72, 576),
        "gu": (2, D, D),
        "gd": (2, 2304, 576),
    }
    half = tokens.shape[0]
    rows = 2 * half
    out_shape, out_specs = [], []

    def out(shape, dtype, space=ANY):
        out_shape.append(jax.ShapeDtypeStruct(shape, dtype))
        out_specs.append(pl.BlockSpec(memory_space=space))

    for s in shapes.values():
        out(s, BF)
    out((2, 1, 3456), F32, VM)
    out((16, 128), F32, VM)
    out((half, D), BF)
    out((half, D), BF)
    out((rows, D), BF)
    out((rows, D), BF)
    out((8, rows, 128), BF)
    out((8, rows, 128), BF)
    out((8, 72, rows), BF)
    out((8, 72, rows), F32)
    out((8, 1, rows), F32, VM)
    out((half, D), BF)
    out((half, D), F32)
    out((rows, D), BF)
    out((rows, 2304), BF)
    out((half, D), BF)
    out((half, D), BF)
    out((2, 2304, 576), BF)
    dma = pltpu.SemaphoreType.DMA
    scratch = [
        VM((144, 864), BF),
        VM((72, 576), BF),
        VM((144, D), BF),
        VM((288, 576), BF),
        VM((2, 72, 864), F32),
        VM((72, 864), F32),
        VM((2, 72, D), F32),
        VM((72, D), F32),
        VM((4, 2, 2, 16, 128), F32),
        VM((4, 2, 2, 1, 3456), F32),
        VM((3, 2, 2, 1, 3456), F32),
        VM((2, 2, 1, 3456), F32),
        VM((2, 2, 2, 1, 3456), F32),
        VM((half, D), BF),
        VM((half, D), BF),
        VM((half, D), BF),
        VM((8, 128), F32),
        VM((rows, D), BF),
        VM((rows, D), BF),
        VM((8, rows, 128), BF),
        VM((8, rows, 128), BF),
        VM((8, 72, rows), BF),
        VM((8, 72, rows), F32),
        VM((rows, 576), BF),
        VM((half, D), BF),
        VM((half, D), BF),
        VM((half, D), BF),
        VM((half, D), BF),
        VM((half, D), F32),
        VM((half, D), F32),
        VM((rows, D), BF),
        VM((rows, 2304), BF),
        VM((rows, 2304), BF),
        VM((half, D), BF),
        VM((half, D), BF),
        VM((half, D), BF),
        VM((2, 2, 384, 576), BF),
        VM((1, 14 * D), F32),
        VM((1, 576), F32),
        VM((1, 576), F32),
        VM((1, 2304), F32),
        dma((8,)),
    ]
    n = len(CHUNKS)
    scratch += [dma((n, 4))] * 6 + [dma((n, 4, 2))] * 2 + [dma((n, 4))] * 2
    scratch += [
        dma((4, 7)),
        dma((4, 7)),
        dma((9,)),
        dma((9,)),
        dma((5, 4)),
        dma((5, 4)),
        dma((2, 2)),
        dma((20,)),
        dma((2,)),
    ]
    vm = pl.BlockSpec(memory_space=VM)
    hbm = pl.BlockSpec(memory_space=ANY)
    return pl.pallas_call(
        forward_kernel,
        out_shape=out_shape,
        in_specs=[vm, hbm] + [vm] * 9,
        out_specs=out_specs,
        scratch_shapes=scratch,
        compiler_params=pltpu.CompilerParams(
            collective_id=0, has_side_effects=True, vmem_limit_bytes=60 * 2**20
        ),
        name="forward_block",
    )(tokens, cotangent, bucket, table, *masters, modulate_master, cond, biases)


class Scatter:
    def __init__(self, grads, boxes, outs, sems):
        self.grads, self.outs = grads, outs
        self.pair_box, self.diag_box, self.x_box, self.y_box, self.z_box = boxes
        self.ps, self.pr, self.fs, self.fr, self.xs, self.xr, self.ys, self.yr, self.zs, self.zr = sems
        self.sent = []

    def piece(self, i, flip_y, k, flip_x):
        z, x, c, y = place()
        weight, first, count, _ = CHUNKS[i]
        return piece_at(
            self.grads[weight], weight, 1 - y if flip_y else y, at_z(k), 1 - x if flip_x else x, first, count
        )

    def box(self, boxes, i, n):
        weight, first, count, _ = CHUNKS[i]
        return boxes[weight].at[n, pl.ds(first, count)]

    def send(self, make):
        make().start()
        self.sent.append(make)

    def arrived(self, ref, s, r):
        rdma(ref, ref, s, r, partners()[0]).wait_recv()

    def add(self, target, *others):
        total = target[...]
        for o in others:
            total = total + o[...]
        target[...] = total

    def across(self, i, k, by_y):
        if by_y:
            return rdma(
                self.piece(i, 1, k, 0), self.box(self.y_box, i, k), self.ys.at[i, k], self.yr.at[i, k], partners()[1]
            )
        return rdma(
            self.piece(i, 0, k, 1), self.box(self.x_box, i, k), self.xs.at[i, k], self.xr.at[i, k], partners()[0]
        )

    def start(self, i):
        def to_pair(k):
            return rdma(
                self.piece(i, 1, k ^ 1, 1),
                self.box(self.pair_box, i, k // 2),
                self.ps.at[i, k],
                self.pr.at[i, k],
                partners()[3][1],
            )

        for k in (0, 2):
            self.send(functools.partial(to_pair, k))
        for k in (1, 3):
            for by_y in (0, 1):
                self.send(functools.partial(self.across, i, k, by_y))

    def corner(self, i, k):
        box = self.box(self.pair_box, i, k // 2)
        self.arrived(box, self.ps.at[i, k], self.pr.at[i, k])
        self.add(self.piece(i, 1, k, 1), box)
        spans = parts_of(i, k)

        def part(n):
            return rdma(
                self.piece(i, 1, k, 1).at[pl.ds(*spans[n])],
                self.box(self.diag_box, i, k // 2).at[pl.ds(*spans[n])],
                self.fs.at[i, k, n],
                self.fr.at[i, k, n],
                partners()[1 - n],
            )

        for n in (0, 1):
            if spans[n] is not None:
                self.send(functools.partial(part, n))

    def plane(self, i, k):
        spans = parts_of(i, k)
        for n in (0, 1):
            if spans[n] is not None:
                part = self.box(self.diag_box, i, k // 2).at[pl.ds(*spans[n])]
                self.arrived(part, self.fs.at[i, k, n], self.fr.at[i, k, n])
                self.add(self.piece(i, n, k, 1 - n).at[pl.ds(*spans[n])], part)
            self.send(functools.partial(self.across, i, k, n))

    def both(self, i, k):
        boxes = []
        for boxes_of, s, r in ((self.x_box, self.xs, self.xr), (self.y_box, self.ys, self.yr)):
            box = self.box(boxes_of, i, k)
            self.arrived(box, s.at[i, k], r.at[i, k])
            boxes.append(box)
        return boxes

    def column(self, i, k):
        self.add(self.piece(i, 0, k, 0), *self.both(i, k))

        def along():
            return rdma(
                self.piece(i, 0, k, 0),
                self.box(self.z_box, i, k - 1),
                self.zs.at[i, k],
                self.zr.at[i, k],
                partners()[3][k],
            )

        self.send(along)

    def last(self, i):
        weight, first, count, _ = CHUNKS[i]
        boxes = self.both(i, 0)
        for k in (1, 2, 3):
            box = self.box(self.z_box, i, k - 1)
            self.arrived(box, self.zs.at[i, k], self.zr.at[i, k])
            boxes.append(box)
        total = self.piece(i, 0, 0, 0)[...].astype(F32)
        for box in boxes:
            total = total + box[...].astype(F32)
        self.outs[weight][first : first + count, :] = total

    def finish(self):
        for make in self.sent:
            make().wait_send()

    def steps(self, i):
        return (
            [(self.start, i), (self.corner, i, 0), (self.corner, i, 2)],
            [(self.plane, i, 0), (self.plane, i, 2), (self.column, i, 1)],
            [(self.column, i, 3), (self.column, i, 2)],
            [(self.last, i)],
        )


def total_steps(dm, bs, lhs, mods, bufs, gmod, bias_out, s, r):
    got_m, got_b, sb, got_z, near = bufs

    def hop(i):
        z, x, c, y = place()
        zn = partners()[3]
        pairs = []
        if i == 0:
            for f in range(1, 8):
                to = flipped(f)
                pairs.append((dm.at[to[3]], got_m.at[x, c, y], to))
                pairs.append((bs, got_b.at[f - 1], to))
        elif i == 1:
            for k in (1, 2, 3):
                pairs.append((mods.at[z], mods.at[z], zn[k]))
                pairs.append((sb, got_z.at[k - 1], zn[k]))
        else:
            pairs.append((near.at[0], near.at[1], flipped(4)))
        return [
            rdma(src, dst, s.at[i, n], r.at[i, n], to) for n, (src, dst, to) in enumerate(pairs)
        ]

    def step(i):
        z, x, c, y = place()
        if i > 0:
            for d in hop(i - 1):
                d.wait()
        if i == 0:
            got_m[x, c, y] = dm[y]
        elif i == 1:
            for n in range(4):
                mods[z, n // 2, n % 2] = rounded(got_m[n // 2, 0, n % 2] + got_m[n // 2, 1, n % 2])
            sb[...] = ((bs[...] + got_b[0]) + (got_b[1] + got_b[2])) + (
                (got_b[3] + got_b[4]) + (got_b[5] + got_b[6])
            )
        elif i == 2:
            rows = [mods[n // 4, n // 2 % 2, n % 2] for n in range(16)]
            total = rows[0]
            for row in rows[1:]:
                total = total + row
            near[0] = total
        elif i == 3:
            for n in (0, 1):
                bias_out[:, n * 3456 : (n + 1) * 3456] = jnp.where(y == n, near[0], near[1])
        if i < 3:
            for d in hop(i):
                d.start()
        if i == 2:
            bias_out[:, 6 * D :] = (sb[...] + got_z[0]) + (got_z[1] + got_z[2])
            left = lhs[:, :72].astype(BF)
            right = jnp.concatenate(rows, axis=0).astype(BF)
            for j in range(3):
                cols = slice(j * D, (j + 1) * D)
                gmod[:, cols] = matmul_tn(left, right[:, cols])

    return [functools.partial(step, i) for i in range(4)]


BEATS = {
    "down": "010101",
    "expand": "010101",
    "up": "010101",
    "middle": "1010",
    "project": "1010",
    "heads": "0001",
    "attend": "010101",
    "back": "000111",
    "input": "1111",
    "hops": "111111",
}


def backward_kernel(*refs):
    gq, gp, gu, gd, mod, lhs = refs[:6]
    (x0_in, dy_in, cl_in, h1_in, q_in, k_in, v_in, at_in, lse) = refs[6:15]
    (ba_in, x1_in, h2_in, der_in, bb_in, y_in, gred) = refs[15:22]
    (out, ig_out, s_att, s_proj, s_exp, s_red, gmod, bias_out, norm_out) = refs[22:31]
    grads = refs[31:35]
    boxes = [refs[35 + 4 * i : 39 + 4 * i] for i in range(5)]
    fq, fu, gotq, gotu = refs[55:59]
    dba, dx1, ps, pr, dm, bs, mods = refs[59:66]
    total_bufs = refs[66:71]
    sq, here = refs[71:73]
    lsem = refs[73]
    scatter_sems = refs[74:84]
    ts, tr, ws, wr, hs, hr, ns, nr = refs[84:92]
    z, x, c, y = place()
    xn, yn, twin, zn = partners()
    half = dx1.shape[0]
    mine = pl.multiple_of(c * half, half)
    other = pl.multiple_of((1 - c) * half, half)
    scatter = Scatter(grads, boxes, (fq, s_proj, fu, s_red), scatter_sems)
    hops = total_steps(dm, bs, lhs, mods, total_bufs, gmod, bias_out, hs, hr)
    pltpu.make_async_copy(gred, grads[3], lsem.at[0]).start()
    dm[...] = jnp.zeros_like(dm)
    bs[...] = jnp.zeros_like(bs)
    TILE = 128
    swap_to = (z, x, y, c)

    def vec(i):
        return mod[i // 3, :, (i % 3) * D : (i % 3 + 1) * D]

    def add_mod(i, value):
        cols = slice((i % 3) * D, (i % 3 + 1) * D)
        dm[i // 3, :, cols] = dm[i // 3, :, cols] + jnp.sum(value, axis=0, keepdims=True)

    def add_bias(at, value):
        cols = slice(at, at + value.shape[1])
        bs[:, cols] = bs[:, cols] + value

    def load(src, dst, i):
        d = pltpu.make_async_copy(src, dst, lsem.at[i])
        d.start()
        return d

    queue = []

    def tick(n):
        for _ in range(min(n, len(queue))):
            f, *a = queue.pop(0)
            f(*a)

    def beat(where, n):
        tick(int(BEATS[where][n]))

    def moves(i):
        if i == 0:
            return y_in, out
        rows = pl.ds((i - 1) * TILE, TILE)
        return dba.at[rows], ig_out.at[rows]

    def move(i):
        @pl.when(c != y)
        def _():
            rdma(*moves(i), ws.at[i], wr.at[i], swap_to).start()

        @pl.when(c == y)
        def _():
            pltpu.make_async_copy(*moves(i), ws.at[i]).start()

    def moved(i):
        @pl.when(c != y)
        def _():
            rdma(*moves(i), ws.at[i], wr.at[i], swap_to).wait()

        @pl.when(c == y)
        def _():
            pltpu.make_async_copy(*moves(i), ws.at[i]).wait()

    def begin():
        greet()
        pltpu.make_async_copy(gred, grads[3], lsem.at[0]).wait()
        scatter.start(5)
        scatter.start(6)
        five, six = scatter.steps(5), scatter.steps(6)
        queue.extend(five[0][1:] + six[0][1:] + five[1] + six[1] + five[2] + six[2] + five[3] + six[3])

    def own_tile(ref, t):
        return ref.at[pl.ds(pl.multiple_of(mine + t * TILE, TILE), TILE)]

    def widen(du):
        def through(weight, closing, der):
            loads = [load(gd, weight, 1), load(cl_in, closing, 2)]

            def slopes(n):
                return load(der_in.at[:, pl.ds(n * 384, 384)], der.at[n % 2], 3 + n % 2)

            coming = slopes(0)
            begin()
            for d in loads:
                d.wait()
            for n in range(6):
                cols = slice(n * 384, (n + 1) * 384)
                coming.wait()
                if n < 5:
                    coming = slopes(n + 1)
                right = jnp.concatenate([weight[0, cols, :], weight[1, cols, :]], axis=1)
                value = (matmul_nt(closing[...], right) * der[n % 2].astype(F32)).astype(BF)
                du[:, cols] = value
                sums = jnp.sum(value.astype(F32), axis=0, keepdims=True)
                here[:, cols] = sums
                beat("down", n)
            for j in range(8):
                block = here[:, j * BLOCK : (j + 1) * BLOCK]
                for p in (0, 1):
                    add_bias(3 * D + (2 * j + p) * BLOCK, jnp.where(c == p, block, 0.0))

        pl.run_scoped(through, VM((2, 2304, 576), BF), VM((2 * half, D), BF), VM((2, 2 * half, 384), BF))

        def expand(weight, h2):
            load(h2_in, h2, 2).wait()
            weight_load = load(gu, weight, 1)
            for t in range(3):
                left = h2[:, t * 384 : (t + 1) * 384].T
                for i in (0, 1):
                    grads[2][i, t * 384 : (t + 1) * 384, :] = matmul(
                        left, du[:, i * D : (i + 1) * D]
                    ).astype(BF)
                    beat("expand", 2 * t + i)

            scatter.start(3)
            scatter.start(4)
            three, four = scatter.steps(3), scatter.steps(4)
            queue.extend(
                three[0][1:] + four[0][1:] + three[1] + four[1] + three[2] + four[2] + three[3] + four[3]
            )
            move(0)

            def product(start, n):
                rows = pl.ds(start, half)
                part = slice(n * 384, (n + 1) * 384)
                return matmul_nt(du[rows, :D], weight[0, part, :]) + matmul_nt(du[rows, D:], weight[1, part, :])

            weight_load.wait()

            for n in range(3):
                ps[:, n * 384 : (n + 1) * 384] = product(other, n).astype(BF)
                beat("up", n)
            rdma(ps, pr, ts.at[0, 0], tr.at[0, 0], twin).start()
            for n in range(3):
                dx1[:, n * 384 : (n + 1) * 384] = product(mine, n)
                beat("up", 3 + n)

        pl.run_scoped(expand, VM((2, D, D), BF), VM((2 * half, D), BF))

    pl.run_scoped(widen, VM((2 * half, 2304), BF))

    def sums_got(i):
        rdma(ps, pr, ts.at[i, 0], tr.at[i, 0], twin).wait()

    def norm_back(value, scaling, gradient):
        average = jnp.mean(value, axis=-1, keepdims=True)
        centred = value - average
        inverse = lax.rsqrt(jnp.mean(centred * centred, axis=-1, keepdims=True) + 1e-06)
        normed = centred * inverse
        inner = gradient * (1.0 + scaling)
        part = inner - jnp.mean(inner, axis=-1, keepdims=True)
        part = part - normed * jnp.mean(inner * normed, axis=-1, keepdims=True)
        return part * inverse, normed

    def middle(x1, dy, ba, bb):
        loads = [load(x1_in, x1, 1), load(dy_in, dy, 2), load(ba_in, ba, 3), load(bb_in, bb, 4)]
        for d in loads:
            d.wait()
        sums_got(0)
        for t in range(half // TILE):
            rows = slice(t * TILE, (t + 1) * TILE)
            gradient = dx1[rows, :] + pr[rows, :].astype(F32)
            part, normed = norm_back(x1[rows, :], vec(4), gradient)
            add_mod(3, gradient)
            add_mod(4, gradient * normed)
            outer = dy[rows, :].astype(F32)
            add_mod(5, outer * bb[rows, :].astype(F32))
            add_bias(9216 - D, jnp.sum(rounded(outer * vec(5)), axis=0, keepdims=True))
            total = outer + part
            dx1[rows, :] = total
            add_mod(2, total * ba[rows, :].astype(F32))
            branch = (total * vec(2)).astype(BF)
            own_tile(dba, t)[...] = branch
            tile = own_tile(dba, t)
            rdma(tile, tile, ts.at[1, t], tr.at[1, t], twin).start()
            add_bias(2 * D, jnp.sum(branch.astype(F32), axis=0, keepdims=True))
            beat("middle", t)

    pl.run_scoped(middle, VM((half, D), F32), VM((half, D), BF), VM((half, D), BF), VM((half, D), BF))

    def attention(dot, dqkv):
        def project(weight, stage, raw, attnt, attn):
            loads = [load(gp, raw, 1), load(at_in, attnt, 2)]
            for d in loads:
                d.wait()
            for i in (0, 1):
                for h in range(8):
                    stage[h * 72 : h * 72 + 72, :] = raw[i, h].astype(F32)
                weight[i] = stage[...].astype(BF)
            attn[...] = jnp.concatenate([attnt[h] for h in range(8)], axis=0).astype(BF)
            for t in range(half // TILE):
                tile = own_tile(dba, t)
                rdma(tile, tile, ts.at[1, t], tr.at[1, t], twin).wait_send()
                part = dba.at[pl.ds(pl.multiple_of(other + t * TILE, TILE), TILE)]
                rdma(part, part, ts.at[1, t], tr.at[1, t], twin).wait_recv()
            for n in range(4):
                rows = slice(n * 256, (n + 1) * 256)
                right = dba[rows, :]
                value = matmul_nt(weight[0], right[:, :576]) + matmul_nt(weight[1], right[:, 576:])
                for h in range(8):
                    dot[h, :, rows] = value[h * 72 : h * 72 + 72, :].astype(BF)
                beat("project", n)
            for i in (0, 1):
                stage[...] = matmul(attn[...], dba[:, i * 576 : (i + 1) * 576])
                for h in range(8):
                    grads[1][i, h] = stage[h * 72 : h * 72 + 72, :].astype(BF)

        pl.run_scoped(
            project,
            VM((2, 576, 576), BF),
            VM((576, 576), F32),
            VM((2, 8, 72, 576), BF),
            VM((8, 72, 2 * half), F32),
            VM((576, 2 * half), BF),
        )
        scatter.start(2)
        two = scatter.steps(2)
        queue.extend(two[0][1:] + two[1] + two[2] + two[3])

        def heads(qa, ka, vt, at, dk, dv, dq):
            def fetch(h):
                n = h % 2
                return [
                    load(src.at[h], dst.at[n], 1 + 4 * n + m)
                    for m, (src, dst) in enumerate(((q_in, qa), (k_in, ka), (v_in, vt), (at_in, at)))
                ]

            coming = fetch(0)
            for h in range(8):
                n = h % 2
                for d in coming:
                    d.wait()
                if h < 7:
                    coming = fetch(h + 1)
                value = vt[n].T
                key_t = ka[n, :, :72].T
                inner = jnp.sum(at[n] * dot[h].astype(F32), axis=0, keepdims=True)
                dk[...] = jnp.zeros_like(dk)
                dv[...] = jnp.zeros_like(dv)
                for i in range(4):
                    rows = slice(i * 256, (i + 1) * 256)
                    query = qa[n, rows, :]
                    grad = dot[h, :, rows]
                    scores = matmul_nt(ka[n], query)
                    prob = jnp.exp2(scores - lse[h, :, rows])
                    change = matmul(value, grad) - inner[:, rows]
                    dscore = (prob * change).astype(BF)
                    dv[...] += matmul_nt(grad, prob.astype(BF))
                    dk[...] += matmul_nt(query[:, :72].T, dscore)
                    dq[:, rows] = matmul(key_t, dscore)
                    beat("heads", i)
                scale = HEAD_DIM ** (-0.5)
                dqkv[0, :, h * 72 : h * 72 + 72] = (dq[...] * scale).T.astype(BF)
                key_grad = (dk[...] * math.log(2.0)).T.astype(BF)
                if h < 4:
                    dqkv[0, :, 576 + h * 72 : 648 + h * 72] = key_grad
                else:
                    dqkv[1, :, h * 72 - 288 : h * 72 - 216] = key_grad
                dqkv[1, :, 288 + h * 72 : 360 + h * 72] = dv[...].T.astype(BF)

        pl.run_scoped(
            heads,
            VM((2, 2 * half, 128), BF),
            VM((2, 2 * half, 128), BF),
            VM((2, 72, 2 * half), BF),
            VM((2, 72, 2 * half), F32),
            VM((72, 2 * half), F32),
            VM((72, 2 * half), F32),
            VM((72, 2 * half), F32),
        )

        def attend(weight, x0):
            loads = [load(gq, weight, 2), load(x0_in, x0, 3)]
            pl.run_scoped(attend_grad, VM((2 * half, D), BF))
            scatter.start(0)
            scatter.start(1)
            zero, one = scatter.steps(0), scatter.steps(1)
            queue.extend(
                zero[0][1:] + one[0][1:] + zero[1] + one[1] + zero[2] + one[2] + zero[3] + one[3]
            )
            for d in loads:
                d.wait()
            pl.run_scoped(functools.partial(back, weight, x0), VM((half, D), F32))

        def attend_grad(h1):
            load(h1_in, h1, 1).wait()
            for t in range(3):
                left = h1[:, t * 384 : (t + 1) * 384].T
                for i in (0, 1):
                    grads[0][i, t * 384 : (t + 1) * 384, :] = matmul(left, dqkv[i]).astype(BF)
                    beat("attend", 2 * t + i)

        def back(weight, x0, acc):
            def product(start, n):
                rows = pl.ds(start, half)
                part = slice(n * 384, (n + 1) * 384)
                return matmul_nt(dqkv[0, rows, :], weight[0, part, :]) + matmul_nt(
                    dqkv[1, rows, :], weight[1, part, :]
                )

            for n in range(3):
                ps[:, n * 384 : (n + 1) * 384] = product(other, n).astype(BF)
                beat("back", n)
            rdma(ps, pr, ts.at[2, 0], tr.at[2, 0], twin).start()
            for n in range(3):
                acc[:, n * 384 : (n + 1) * 384] = product(mine, n)
                beat("back", 3 + n)
            sums_got(2)
            for t in range(half // TILE):
                rows = slice(t * TILE, (t + 1) * TILE)
                gradient = acc[rows, :] + pr[rows, :].astype(F32)
                part, normed = norm_back(x0[rows, :].astype(F32), vec(1), gradient)
                add_mod(0, gradient)
                add_mod(1, gradient * normed)
                dba[rows, :] = (dx1[rows, :] + part).astype(BF)
                move(1 + t)
                beat("input", t)

        pl.run_scoped(
            attend,
            VM((2, D, 864), BF),
            VM((half, D), BF),
        )
        for i in (0, 1):
            sums = jnp.sum(dqkv[i].astype(F32), axis=0, keepdims=True)
            for j in range(8):
                block = sums[:, i * 288 + j * 72 : i * 288 + j * 72 + 72]
                for p in (0, 1):
                    add_bias(i * D + (2 * j + p) * 72, jnp.where(c == p, block, 0.0))

    pl.run_scoped(attention, VM((8, 72, 2 * half), BF), VM((2, 2 * half, 864), BF))
    for n, hop in enumerate(hops):
        hop()
        beat("hops", n)
    tick(len(queue))

    last_half = 72
    def give(f, got, i):
        return rdma(f.at[pl.ds(pl.multiple_of((1 - c) * 72, 8), 72)], got, ts.at[3, i], tr.at[3, i], twin)

    give(fq, gotq, 0).start()
    give(fu, gotu, 1).start()

    def squares(value):
        return jnp.sum(jnp.sum(value * value, axis=0, keepdims=True), axis=1, keepdims=True)

    bias_squares = squares(bias_out[...])
    total = squares(fq[...]) + squares(fu[...]) + squares(s_proj[...]) + squares(s_red[...]) + squares(gmod[...])
    total = jnp.broadcast_to(total, (8, 128))
    sq[0] = total
    near = [
        rdma(sq.at[0], sq.at[f], ns.at[f - 1], nr.at[f - 1], flipped(f)) for f in range(1, 8)
    ]
    for d in near:
        d.start()
    for d in near:
        d.wait()
    sq[8] = ((sq[0] + sq[1]) + (sq[2] + sq[3])) + ((sq[4] + sq[5]) + (sq[6] + sq[7]))
    last = [rdma(sq.at[8], sq.at[8 + k], ns.at[6 + k], nr.at[6 + k], zn[k]) for k in (1, 2, 3)]
    for d in last:
        d.start()

    def interleave(f, got, shard, width, i):
        give(f, got, i).wait()
        own = jnp.where(c == 0, f[:72, :], f[72:, :])
        sides = (jnp.where(c == 0, own, got[...]), jnp.where(c == 0, got[...], own))
        count = own.shape[1] // width
        shard[...] = jnp.concatenate(
            [sides[p][:, j * width : (j + 1) * width] for j in range(count) for p in (0, 1)], axis=1
        )

    interleave(fq, gotq, s_att, HEAD_DIM, 0)
    interleave(fu, gotu, s_exp, BLOCK, 1)
    for d in last:
        d.wait()
    norm_out[...] = (sq[8] + sq[9]) + (sq[10] + sq[11]) + bias_squares
    for i in range(1 + half // TILE):
        moved(i)
    scatter.finish()


def backward_block(kept):
    half = kept[6].shape[0]
    rows = 2 * half
    sd = jax.ShapeDtypeStruct
    vm = pl.BlockSpec(memory_space=VM)
    hbm = pl.BlockSpec(memory_space=ANY)
    sizes = ((D, 864), (72, 576), (D, D), (2304, 576))
    pieces = [PIECES[n][:2] for n in NAMES]
    dma = pltpu.SemaphoreType.DMA
    n = len(CHUNKS)
    scratch = [
        VM((2, D, 864), BF),
        VM((2, 8, 72, 576), BF),
        VM((2, D, D), BF),
        VM((2, 2304, 576), BF),
    ]
    for count in (2, 2, 4, 4, 3):
        scratch += [VM((count,) + p, BF) for p in pieces]
    scratch += [
        VM((144, 864), F32),
        VM((144, D), F32),
        VM((72, 864), F32),
        VM((72, D), F32),
        VM((rows, D), BF),
        VM((half, D), F32),
        VM((half, D), BF),
        VM((half, D), BF),
        VM((2, 1, 3456), F32),
        VM((1, 9216), F32),
        VM((4, 2, 2, 1, 3456), F32),
        VM((2, 2, 2, 1, 3456), F32),
        VM((7, 1, 9216), F32),
        VM((1, 9216), F32),
        VM((3, 1, 9216), F32),
        VM((2, 1, 3456), F32),
        VM((12, 8, 128), F32),
        VM((1, 2304), F32),
        dma((9,)),
    ]
    scratch += [dma((n, 4))] * 2 + [dma((n, 4, 2))] * 2 + [dma((n, 4))] * 6
    scratch += [dma((4, 4))] * 2 + [dma((5,))] * 2 + [dma((3, 14))] * 2 + [dma((10,))] * 2
    places = [hbm] * 4 + [vm, vm] + [hbm] * 8 + [vm] + [hbm] * 7
    return pl.pallas_call(
        backward_kernel,
        out_shape=[
            sd((half, D), BF),
            sd((half, D), BF),
            sd((72, 1728), F32),
            sd((72, 576), F32),
            sd((72, 2304), F32),
            sd((288, 576), F32),
            sd((72, 3456), F32),
            sd((1, 14 * D), F32),
            sd((8, 128), F32),
        ],
        in_specs=places,
        out_specs=[hbm, hbm] + [vm] * 7,
        scratch_shapes=scratch,
        compiler_params=pltpu.CompilerParams(
            collective_id=1, has_side_effects=True, vmem_limit_bytes=62 * 2**20
        ),
        name="backward_block",
    )(*kept)


def step_kernel(squares, correction, *refs):
    count = len(RATES)
    norm = jnp.sqrt(squares[0:1, 0:1])
    clip = jnp.minimum(1.0, 1.0 / (norm + 1e-06))
    fix = correction[0:1, 0:1]
    for i, rate in enumerate(RATES):
        master, first, second, gradient = (refs[4 * i + j][...] for j in range(4))
        new = adam_update(master, first, second, gradient, rate, clip, fix)
        for j in range(3):
            refs[4 * count + 3 * i + j][...] = new[j]


RATES = (0.5 * D ** (-0.5),) * 4 + (0.5 * FF ** (-0.5),)


def step_weights(squares, correction, states):
    grid = 3

    def spec(shape):
        return pl.BlockSpec((shape[0] // grid, shape[1]), lambda i: (i, 0))

    whole = pl.BlockSpec((8, 128), lambda i: (0, 0))
    flat = [value for state in states for value in state]
    new = [value for state in states for value in state[:3]]
    return pl.pallas_call(
        step_kernel,
        grid=(grid,),
        out_shape=[jax.ShapeDtypeStruct(v.shape, v.dtype) for v in new],
        in_specs=[whole, whole] + [spec(v.shape) for v in flat],
        out_specs=[spec(v.shape) for v in new],
        compiler_params=pltpu.CompilerParams(vmem_limit_bytes=62 * 2**20),
        name="step_weights",
    )(squares, correction, *flat)


def on_device_fast(
    tokens,
    cotangent,
    buckets,
    timesteps,
    labels,
    class_table,
    step_count,
    modulate_master,
    modulate_first,
    modulate_second,
    attend_master,
    attend_first,
    attend_second,
    project_master,
    project_first,
    project_second,
    expand_master,
    expand_first,
    expand_second,
    reduce_master,
    reduce_first,
    reduce_second,
    biases_master,
    biases_first,
    biases_second,
):

    z, x, c, y = place()
    bf16, f32 = jnp.bfloat16, jnp.float32
    block = FF // 16
    class_row = lax.dynamic_slice_in_dim(class_table, labels[0], 1).astype(f32)
    condition = jax.nn.silu(class_row + time_features(timesteps, D)).astype(bf16).astype(f32)
    cond_tiles = jnp.pad(condition.reshape(16, 72), ((0, 0), (0, 56)))
    bucket = jnp.broadcast_to(buckets.astype(f32)[:, None], (8, 128))
    steps = jnp.arange(64, dtype=f32)[:, None]
    omegas = jnp.exp(-math.log(10000.0) * jnp.arange(288, dtype=f32) / 288)[None, :]
    table = jnp.concatenate([jnp.sin(steps * omegas), jnp.cos(steps * omegas)], axis=1)
    kept = forward_block(
        tokens,
        cotangent,
        bucket,
        table,
        (attend_master, project_master, expand_master, reduce_master),
        modulate_master,
        cond_tiles,
        biases_master,
    )
    (output, input_grad, grad_attend, grad_project, grad_expand, grad_reduce, grad_mod, bias_total, squares) = (
        backward_block(kept)
    )
    correction = 1.0 - jnp.power(0.5, step_count.astype(f32))
    states = (
        (modulate_master, modulate_first, modulate_second, grad_mod),
        (attend_master, attend_first, attend_second, grad_attend),
        (project_master, project_first, project_second, grad_project),
        (expand_master, expand_first, expand_second, grad_expand),
        (reduce_master, reduce_first, reduce_second, grad_reduce),
    )
    updates = list(step_weights(squares, jnp.full((8, 128), correction), states))
    grad_norm = jnp.sqrt(squares[0, 0])
    clip_factor = jnp.minimum(1.0, 1.0 / (grad_norm + 1e-06))
    updates += adam_update(
        biases_master, biases_first, biases_second, bias_total[0], 0.1, clip_factor, correction
    )
    return (output, input_grad.astype(f32), grad_norm, *updates)


def fast_solution(mesh):
    return jax.shard_map(
        on_device_fast,
        mesh=mesh,
        in_specs=(
            P(("z", "x", "c", "y"), None),
            P(("z", "x", "c", "y"), None),
            P(("z", "x", "c")),
            P(("z", "x", "c")),
            P(("z", "x", "c")),
            P(),
            P(),
            P(("z", "x", "c"), "y"),
            P(("z", "x", "c"), "y"),
            P(("z", "x", "c"), "y"),
            P(("z", "x", "c"), "y"),
            P(("z", "x", "c"), "y"),
            P(("z", "x", "c"), "y"),
            P(("z", "x", "c"), "y"),
            P(("z", "x", "c"), "y"),
            P(("z", "x", "c"), "y"),
            P(("z", "x", "c"), "y"),
            P(("z", "x", "c"), "y"),
            P(("z", "x", "c"), "y"),
            P(("z", "x", "c"), "y"),
            P(("z", "x", "c"), "y"),
            P(("z", "x", "c"), "y"),
            P(),
            P(),
            P(),
        ),
        out_specs=(
            P(("z", "x", "c", "y"), None),
            P(("z", "x", "c", "y"), None),
            P(),
            P(("z", "x", "c"), "y"),
            P(("z", "x", "c"), "y"),
            P(("z", "x", "c"), "y"),
            P(("z", "x", "c"), "y"),
            P(("z", "x", "c"), "y"),
            P(("z", "x", "c"), "y"),
            P(("z", "x", "c"), "y"),
            P(("z", "x", "c"), "y"),
            P(("z", "x", "c"), "y"),
            P(("z", "x", "c"), "y"),
            P(("z", "x", "c"), "y"),
            P(("z", "x", "c"), "y"),
            P(("z", "x", "c"), "y"),
            P(("z", "x", "c"), "y"),
            P(("z", "x", "c"), "y"),
            P(),
            P(),
            P(),
        ),
        check_vma=False,
    )


def plain_solution(mesh):
    return jax.shard_map(
        on_device,
        mesh=mesh,
        in_specs=(
            P(("seq", "head"), None),
            P(("seq", "head"), None),
            P("seq"),
            P("seq"),
            P("seq"),
            P(),
            P(),
            P("seq", "head"),
            P("seq", "head"),
            P("seq", "head"),
            P("seq", "head"),
            P("seq", "head"),
            P("seq", "head"),
            P("seq", "head"),
            P("seq", "head"),
            P("seq", "head"),
            P("seq", "head"),
            P("seq", "head"),
            P("seq", "head"),
            P("seq", "head"),
            P("seq", "head"),
            P("seq", "head"),
            P(),
            P(),
            P(),
        ),
        out_specs=(
            P(("seq", "head"), None),
            P(("seq", "head"), None),
            P(),
            P("seq", "head"),
            P("seq", "head"),
            P("seq", "head"),
            P("seq", "head"),
            P("seq", "head"),
            P("seq", "head"),
            P("seq", "head"),
            P("seq", "head"),
            P("seq", "head"),
            P("seq", "head"),
            P("seq", "head"),
            P("seq", "head"),
            P("seq", "head"),
            P("seq", "head"),
            P("seq", "head"),
            P(),
            P(),
            P(),
        ),
        check_vma=False,
    )


def solution(mesh):
    if dict(mesh.shape) == {"seq": 16, "head": 2}:
        grid = Mesh(mesh.devices.reshape(4, 2, 2, 2), ("z", "x", "c", "y"))
        return fast_solution(grid)
    return plain_solution(mesh)
```

profile of v0, /device:TPU:0, one launch (start us, length us, event | category | flops | bytes accessed | tf_op | source)
XLA Modules:
  0.0 429.5 jit_solution(16380679383274726170)
XLA Ops:
  2.0 0.1 fusion.3
  2.1 0.8 convert_reduce_fusion
  2.9 0.1 reshape.81
  3.0 0.6 pad_convert_fusion.refs_9_
  3.6 0.4 fusion.1
  4.0 0.8 pad_maximum_fusion.refs_3_
  5.4 0.6 broadcast_in_dim.7.refs_2_
  6.0 197.3 %forward_block.1 = (bf16[2,1152,864]{2,1,0:T(8,128)(2,1)}, bf16[2,8,72,576]{3,2,1,0:T(8,128)(2,1)}, bf16[2,1152,1152]{2,1,0:T(8,128)(2,1)}, bf16[2,2304,576]{2,1...) custom-call(bf16[512,1152]{1,0:T(8,128)(2,1)} %refs_0_.2, ...), custom_call_target="tpu_custom_call" | custom-call | tf_op jit(solution)/shard_map/forward_block/pallas_call | solution.py:1251
  203.3 0.0 copy-start.2
  203.3 0.0 copy-start.3
  203.4 0.0 copy-start.4
  203.4 207.9 %backward_block.1 = (bf16[512,1152]{1,0:T(8,128)(2,1)}, bf16[512,1152]{1,0:T(8,128)(2,1)}, f32[72,1728]{1,0:T(8,128)}, f32[72,576]{1,0:T(8,128)}, f32[72,2304]{1...) custom-call(bf16[2,1152,864]{2,1,0:T(8,128)(2,1)} %get-tuple-element.67.refs_0_, ...), custom_call_target="tpu_custom_call" | custom-call | tf_op jit(solution)/shard_map/backward_block/pallas_call | solution.py:1904
  411.3 1.2 slice.3
  413.2 1.0 multiply_reduce_fusion
  414.9 0.0 copy-done.2
  414.9 0.0 copy-done.3
  414.9 0.0 copy-done.4
  414.9 0.7 multiply_subtract_fusion
  415.6 0.6 broadcast_in_dim.8.correction
  416.2 0.0 copy-start
  416.2 9.2 %step_weights.1 = (f32[72,3456]{1,0:T(8,128)}, f32[72,3456]{1,0:T(8,128)}, f32[72,3456]{1,0:T(8,128)}, f32[72,1728]{1,0:T(8,128)}, f32[72,1728]{1,0:T(8,128)}, /...) custom-call(f32[8,128]{1,0:T(8,128)} %get-tuple-element.91.squares, ...), custom_call_target="tpu_custom_call" | custom-call | tf_op jit(solution)/shard_map/step_weights/pallas_call | solution.py:1951
  425.5 0.0 copy-start.1
  425.5 0.0 copy-done
  425.5 1.6 convert_element_type.25
  427.0 0.1 copy-done.1
  427.1 1.0 copy.51
  (1 shorter events, 0.0 us)
Async XLA Ops:
  203.3 211.6 %copy-start.2 = (f32[16128]{0:T(1024)S(1)}, f32[16128]{0:T(1024)}, u32[]{:S(2)}) copy-start(f32[16128]{0:T(1024)} %refs_10_.2) | copy-start | bytes 193540
  203.3 211.6 %copy-start.3 = (f32[16128]{0:T(1024)S(1)}, f32[16128]{0:T(1024)}, u32[]{:S(2)}) copy-start(f32[16128]{0:T(1024)} %param.49) | copy-start | bytes 193540
  203.4 211.6 %copy-start.4 = (f32[16128]{0:T(1024)S(1)}, f32[16128]{0:T(1024)}, u32[]{:S(2)}) copy-start(f32[16128]{0:T(1024)} %param.48) | copy-start | bytes 193540
  416.2 9.2 %copy-start = (bf16[512,1152]{1,0:T(8,128)(2,1)S(1)}, bf16[512,1152]{1,0:T(8,128)(2,1)}, u32[]{:S(2)}) copy-start(bf16[512,1152]{1,0:T(8,128)(2,1)} %get-tuple-element.90) | copy-start | bytes 3538948
  425.5 1.7 copy-start.1
where the time goes:
time: 438 us; the launch traced here: 429 us
  Pallas kernels  414 us (95%)
  other arithmetic  5.95 us (1%)
  between operations  5.45 us (1%)
    pallas_call x1, Pallas kernels, backward_block(): pl.pallas_call(backward_kernel, out_shape=[sd((half, D), BF), sd((half, D...  208 us
    pallas_call x1, Pallas kernels, forward_block(): pl.pallas_call(forward_kernel, out_shape=out_shape, in_specs=[vm, hbm] +...  197 us
    pallas_call x1, Pallas kernels, step_weights(): pl.pallas_call(step_kernel, grid=(grid,), out_shape=[jax.ShapeDtypeStruct...  9.22 us

commit v1 on v0

--- a/solution.py
+++ b/solution.py
@@ -1468,16 +1468,16 @@
     gq, gp, gu, gd, mod, lhs = refs[:6]
     (x0_in, dy_in, cl_in, h1_in, q_in, k_in, v_in, at_in, lse) = refs[6:15]
     (ba_in, x1_in, h2_in, der_in, bb_in, y_in, gred) = refs[15:22]
-    (out, ig_out, s_att, s_proj, s_exp, s_red, gmod, bias_out, norm_out) = refs[22:31]
+    (out, ig_out, s_att, s_proj, s_exp, s_red, gmod, bias_flat, norm_out) = refs[22:31]
     grads = refs[31:35]
     boxes = [refs[35 + 4 * i : 39 + 4 * i] for i in range(5)]
     fq, fu, gotq, gotu = refs[55:59]
     dba, dx1, ps, pr, dm, bs, mods = refs[59:66]
     total_bufs = refs[66:71]
-    sq, here = refs[71:73]
-    lsem = refs[73]
-    scatter_sems = refs[74:84]
-    ts, tr, ws, wr, hs, hr, ns, nr = refs[84:92]
+    sq, here, bias_out = refs[71:74]
+    lsem = refs[74]
+    scatter_sems = refs[75:85]
+    ts, tr, ws, wr, hs, hr, ns, nr = refs[85:93]
     z, x, c, y = place()
     xn, yn, twin, zn = partners()
     half = dx1.shape[0]
@@ -1825,6 +1825,7 @@
         return jnp.sum(jnp.sum(value * value, axis=0, keepdims=True), axis=1, keepdims=True)
 
     bias_squares = squares(bias_out[...])
+    bias_flat[...] = bias_out[...].reshape(14 * D)
     total = squares(fq[...]) + squares(fu[...]) + squares(s_proj[...]) + squares(s_red[...]) + squares(gmod[...])
     total = jnp.broadcast_to(total, (8, 128))
     sq[0] = total
@@ -1896,6 +1897,7 @@
         VM((2, 1, 3456), F32),
         VM((12, 8, 128), F32),
         VM((1, 2304), F32),
+        VM((1, 14 * D), F32),
         dma((9,)),
     ]
     scratch += [dma((n, 4))] * 2 + [dma((n, 4, 2))] * 2 + [dma((n, 4))] * 6
@@ -1911,7 +1913,7 @@
             sd((72, 2304), F32),
             sd((288, 576), F32),
             sd((72, 3456), F32),
-            sd((1, 14 * D), F32),
+            sd((14 * D,), F32),
             sd((8, 128), F32),
         ],
         in_specs=places,
@@ -1933,13 +1935,22 @@
         master, first, second, gradient = (refs[4 * i + j][...] for j in range(4))
         new = adam_update(master, first, second, gradient, rate, clip, fix)
         for j in range(3):
-            refs[4 * count + 3 * i + j][...] = new[j]
+            refs[4 * count + 4 + 3 * i + j][...] = new[j]
+
+    @pl.when(pl.program_id(0) == 0)
+    def _():
+        master, first, second, gradient = (
+            refs[4 * count + j][...].reshape(1, 14 * D) for j in range(4)
+        )
+        new = adam_update(master, first, second, gradient, 0.1, clip, fix)
+        for j in range(3):
+            refs[7 * count + 4 + j][...] = new[j].reshape(14 * D)
 
 
 RATES = (0.5 * D ** (-0.5),) * 4 + (0.5 * FF ** (-0.5),)
 
 
-def step_weights(squares, correction, states):
+def step_weights(squares, correction, states, biases):
     grid = 3
 
     def spec(shape):
@@ -1947,16 +1958,17 @@
 
     whole = pl.BlockSpec((8, 128), lambda i: (0, 0))
     flat = [value for state in states for value in state]
-    new = [value for state in states for value in state[:3]]
+    new = [value for state in states for value in state[:3]] + list(biases[:3])
+    line = pl.BlockSpec(biases[0].shape, lambda i: (0,))
     return pl.pallas_call(
         step_kernel,
         grid=(grid,),
         out_shape=[jax.ShapeDtypeStruct(v.shape, v.dtype) for v in new],
-        in_specs=[whole, whole] + [spec(v.shape) for v in flat],
-        out_specs=[spec(v.shape) for v in new],
+        in_specs=[whole, whole] + [spec(v.shape) for v in flat] + [line] * 4,
+        out_specs=[spec(v.shape) for v in new[:-3]] + [line] * 3,
         compiler_params=pltpu.CompilerParams(vmem_limit_bytes=62 * 2**20),
         name="step_weights",
-    )(squares, correction, *flat)
+    )(squares, correction, *flat, *biases)
 
 
 def on_device_fast(
@@ -2018,12 +2030,13 @@
         (expand_master, expand_first, expand_second, grad_expand),
         (reduce_master, reduce_first, reduce_second, grad_reduce),
     )
-    updates = list(step_weights(squares, jnp.full((8, 128), correction), states))
+    updates = step_weights(
+        squares,
+        jnp.full((8, 128), correction),
+        states,
+        (biases_master, biases_first, biases_second, bias_total),
+    )
     grad_norm = jnp.sqrt(squares[0, 0])
-    clip_factor = jnp.minimum(1.0, 1.0 / (grad_norm + 1e-06))
-    updates += adam_update(
-        biases_master, biases_first, biases_second, bias_total[0], 0.1, clip_factor, correction
-    )
     return (output, input_grad.astype(f32), grad_norm, *updates)
 
 

time: 438 us -> 438 us (level)
  no operation moved by 1% of the time
where the time goes in v1:
time: 438 us; the launch traced here: 429 us
  Pallas kernels  416 us (95%)
  between operations  5.37 us (1%)
    pallas_call x1, Pallas kernels, backward_block(): pl.pallas_call(backward_kernel, out_shape=[sd((half, D), BF), sd((half, D...  208 us
    pallas_call x1, Pallas kernels, forward_block(): pl.pallas_call(forward_kernel, out_shape=out_shape, in_specs=[vm, hbm] +...  197 us
    pallas_call x1, Pallas kernels, step_weights(): pl.pallas_call(step_kernel, grid=(grid,), out_shape=[jax.ShapeDtypeStruct...  10.7 us

profile of v1, /device:TPU:0, one launch (start us, length us, event | category | flops | bytes accessed | tf_op | source)
XLA Modules:
  0.0 429.3 jit_solution(10191327368537427719)
XLA Ops:
  2.0 0.1 fusion.2
  2.1 0.8 convert_reduce_fusion
  2.9 0.1 reshape.79
  3.0 0.6 pad_convert_fusion.refs_9_
  3.6 0.4 fusion.1
  4.0 0.8 pad_maximum_fusion.refs_3_
  5.4 0.6 broadcast_in_dim.7.refs_2_
  6.0 197.3 %forward_block.1 = (bf16[2,1152,864]{2,1,0:T(8,128)(2,1)}, bf16[2,8,72,576]{3,2,1,0:T(8,128)(2,1)}, bf16[2,1152,1152]{2,1,0:T(8,128)(2,1)}, bf16[2,2304,576]{2,1...) custom-call(bf16[512,1152]{1,0:T(8,128)(2,1)} %refs_0_.2, ...), custom_call_target="tpu_custom_call" | custom-call | tf_op jit(solution)/shard_map/forward_block/pallas_call | solution.py:1251
  203.3 208.1 %backward_block.1 = (bf16[512,1152]{1,0:T(8,128)(2,1)}, bf16[512,1152]{1,0:T(8,128)(2,1)}, f32[72,1728]{1,0:T(8,128)}, f32[72,576]{1,0:T(8,128)}, f32[72,2304]{1...) custom-call(bf16[2,1152,864]{2,1,0:T(8,128)(2,1)} %get-tuple-element.70.refs_0_, ...), custom_call_target="tpu_custom_call" | custom-call | tf_op jit(solution)/shard_map/backward_block/pallas_call | solution.py:1906
  412.1 0.6 broadcast_in_dim.8.correction
  412.7 0.0 copy-start
  412.7 10.7 %step_weights.1 = (f32[72,3456]{1,0:T(8,128)}, f32[72,3456]{1,0:T(8,128)}, f32[72,3456]{1,0:T(8,128)}, f32[72,1728]{1,0:T(8,128)}, f32[72,1728]{1,0:T(8,128)}, /...) custom-call(f32[8,128]{1,0:T(8,128)} %get-tuple-element.94.squares, ...), custom_call_target="tpu_custom_call" | custom-call | tf_op jit(solution)/shard_map/step_weights/pallas_call | solution.py:1963
  423.4 0.0 copy-start.1
  423.5 0.0 copy-done
  423.5 1.6 convert_element_type.25
  425.0 1.2 slice.3
  426.9 0.0 copy-done.1
  426.9 1.0 copy.51
  (1 shorter events, 0.0 us)
Async XLA Ops:
  412.7 10.7 %copy-start = (bf16[512,1152]{1,0:T(8,128)(2,1)S(1)}, bf16[512,1152]{1,0:T(8,128)(2,1)}, u32[]{:S(2)}) copy-start(bf16[512,1152]{1,0:T(8,128)(2,1)} %get-tuple-element.93) | copy-start | bytes 3538948
  423.4 3.5 copy-start.1
